TPU v7x, 128 devices: a whole 4x4x4 slice. The times are simulated.
128 devices in a mesh: role: 4 (over y), dom: 32 (over x, z, core).
Axes of the slice: x: 4, y: 4, z: 4, core: 2. Of those that a mesh axis runs over, the one named last changes fastest.
Arguments:
- tire_pos: float32 [3, 1572864], P(None, ('role', 'dom')), may hold values from -6 to 6
- tire_vel: float32 [3, 1572864], P(None, ('role', 'dom')), may hold values from -3 to 3
- part_pos: float32 [3, 1048576], P(None, ('role', 'dom')), may hold values from -6 to 6
- part_vel: float32 [3, 1048576], P(None, ('role', 'dom')), may hold values from -3 to 3
- contact_owner: int32 [12288, 2], P(('role', 'dom')), may hold values from 0 to 127, all different within a row; in each aligned block of 96 rows (0 to 95, 96 to 191, ...) at most 2 rows name the same one
- contact_tile: int32 [12288, 2], P(('role', 'dom')), may hold values from 0 to 63
- halo_tiles: int32 [512], P(('role', 'dom')), may hold values from 0 to 63
- block_inverse: float32 [12288, 128, 128], P(('role', 'dom')), may hold values from -1 to 1, as said below
- pattern: int32 [12288, 3], P(('role', 'dom')), may hold values from 0 to 95
- coupling: float32 [12288, 3], P(('role', 'dom')), may hold values from 0.05 to 0.2
Outputs:
- tire_pos_out: float32 [3, 1572864], P(None, ('role', 'dom'))
- tire_vel_out: float32 [3, 1572864], P(None, ('role', 'dom'))
- part_pos_out: float32 [3, 1048576], P(None, ('role', 'dom'))
- part_vel_out: float32 [3, 1048576], P(None, ('role', 'dom'))
Inputs may be any that keep to these rules, and one draw needn't show every extreme that they name: `contact_owner`: among the 96 rows of one device, no owner is named by more than 2 rows, a bound that some block reaches; each row names 2 different owners. `block_inverse`: each block has its diagonal near 0.6.
All inputs are finite; a program needn't handle non-finite values.
Results may differ from a plain program's by a relative error of at most 0.0001.
Values sent between devices are 32-bit elements; how exact they have to be, the bound alone decides.
A program may use at most 64 MiB of HBM per device.

v0:
```python
import jax
import jax.numpy as jnp
from jax import lax
from jax.sharding import PartitionSpec as P

BLK = 128
TOPC = 2
STEPS = 2
SWEEPS = 3


contact_gain = 0.05
soil_gain = 0.05
time_step = 0.1
spread_sq = 4.0


def shifted(shard, axis, by):
    size = lax.axis_size(axis)
    pairs = [(i, i + by) for i in range(size) if 0 <= i + by < size]
    return lax.ppermute(shard, axis, pairs)


def pair_force(near_pos, far_pos, gain, live):
    diff = near_pos[:, :, :, None] - far_pos[:, :, None, :]
    dist = jnp.sum(diff * diff, axis=1)
    weight = gain * jnp.exp(-dist / spread_sq) * live[:, None, None]
    on_near = jnp.einsum("nij,ncj->nci", weight, far_pos, precision=lax.Precision.HIGHEST)
    on_far = jnp.einsum("nij,nci->ncj", weight, near_pos, precision=lax.Precision.HIGHEST)
    push = near_pos * jnp.sum(weight, axis=2)[:, None, :] - on_near
    react = far_pos * jnp.sum(weight, axis=1)[:, None, :] - on_far
    return (push, react)


def outward(send_pos, send_tile):
    return (
        lax.all_to_all(send_pos, ("role", "dom"), split_axis=0, concat_axis=0, tiled=True),
        lax.all_to_all(send_tile, ("role", "dom"), split_axis=0, concat_axis=0, tiled=True),
    )


def inward(pushes):
    return lax.all_to_all(pushes, ("role", "dom"), split_axis=0, concat_axis=0, tiled=True)


def local(
    tire_pos,
    tire_vel,
    part_pos,
    part_vel,
    contact_owner,
    contact_tile,
    halo_tiles,
    block_inverse,
    pattern,
    coupling,
):
    devices = lax.axis_size(("role", "dom"))
    blocks = tire_pos.shape[1] // BLK
    tiles = part_pos.shape[1] // BLK
    pairs = blocks * TOPC
    capacity = max(2, pairs // devices + 1)
    slot_total = devices * capacity
    group = 32
    owner_flat = contact_owner.reshape(-1)
    owner_hot = (owner_flat[:, None] == jnp.arange(devices, dtype=jnp.int32)[None, :]).astype(
        jnp.int32
    )
    earlier = jnp.cumsum(owner_hot, axis=0) - owner_hot
    slot_rank = jnp.sum(owner_hot * earlier, axis=1)
    dest_slot = owner_flat * capacity + slot_rank
    pair_block = jnp.arange(pairs, dtype=jnp.int32) // TOPC
    send_tile = (
        jnp.full((slot_total,), -1, jnp.int32)
        .at[dest_slot]
        .set(contact_tile.reshape(-1))
        .reshape(devices, capacity)
    )
    halo_live = jnp.full((halo_tiles.shape[0],), 1.0, jnp.float32) * (
        lax.axis_index(("role", "dom")) > 0
    ).astype(jnp.float32)
    halo_hot = (jnp.arange(tiles, dtype=jnp.int32)[:, None] == halo_tiles[None, :]).astype(
        jnp.float32
    )
    for step_count in range(STEPS):
        node_blocks = tire_pos.reshape(3, blocks, BLK).transpose(1, 0, 2)
        part_tiles = part_pos.reshape(3, tiles, BLK).transpose(1, 0, 2)
        send_pos = (
            jnp.zeros((slot_total, 3, BLK), jnp.float32).at[dest_slot].set(node_blocks[pair_block])
        )
        recv_pos, recv_tile = outward(send_pos.reshape(devices, capacity, 3, BLK), send_tile)
        recv_pos = recv_pos.reshape(slot_total, 3, BLK)
        recv_tile = recv_tile.reshape(slot_total)
        live = (recv_tile >= 0).astype(jnp.float32)
        far_pos = part_tiles[jnp.maximum(recv_tile, 0)]
        count = slot_total // group

        def one_group(items):
            return pair_force(items[0], items[1], contact_gain, items[2])

        push, react = lax.map(
            one_group,
            (
                recv_pos.reshape(count, group, 3, BLK),
                far_pos.reshape(count, group, 3, BLK),
                live.reshape(count, group),
            ),
        )
        tile_hot = (jnp.arange(tiles, dtype=jnp.int32)[:, None] == recv_tile[None, :]).astype(
            jnp.float32
        )
        soil_force = jnp.dot(
            tile_hot, react.reshape(slot_total, 3 * BLK), precision=lax.Precision.HIGHEST
        )
        pushed = inward(push.reshape(devices, capacity, 3, BLK)).reshape(slot_total, 3, BLK)
        node_force = pushed[dest_slot].reshape(blocks, TOPC, 3, BLK).sum(axis=1)
        edge_pos = part_tiles[halo_tiles]
        incoming = shifted(edge_pos, ("role", "dom"), 1)
        halo_push, unused = pair_force(edge_pos, incoming, soil_gain, halo_live)
        soil_force = soil_force + jnp.dot(
            halo_hot, halo_push.reshape(-1, 3 * BLK), precision=lax.Precision.HIGHEST
        )
        soil_flat = soil_force.reshape(tiles, 3, BLK).transpose(1, 0, 2).reshape(3, -1)
        vel_blocks = tire_vel.reshape(3, blocks, BLK).transpose(1, 0, 2)
        rhs = vel_blocks + time_step * node_force
        velocity = jnp.einsum("bij,bcj->bci", block_inverse, rhs, precision=lax.Precision.HIGHEST)
        for sweep_count in range(SWEEPS):
            coupled = rhs + jnp.sum(coupling[:, :, None, None] * velocity[pattern], axis=1)
            velocity = jnp.einsum(
                "bij,bcj->bci", block_inverse, coupled, precision=lax.Precision.HIGHEST
            )
        part_vel = part_vel + time_step * soil_flat
        part_pos = part_pos + time_step * part_vel
        tire_vel = velocity.transpose(1, 0, 2).reshape(3, -1)
        tire_pos = tire_pos + time_step * tire_vel
    return (tire_pos, tire_vel, part_pos, part_vel)


def solution(mesh):
    return jax.shard_map(
        local,
        mesh=mesh,
        in_specs=(
            P(None, ("role", "dom")),
            P(None, ("role", "dom")),
            P(None, ("role", "dom")),
            P(None, ("role", "dom")),
            P(("role", "dom"), None),
            P(("role", "dom"), None),
            P(("role", "dom")),
            P(("role", "dom"), None, None),
            P(("role", "dom"), None),
            P(("role", "dom"), None),
        ),
        out_specs=(
            P(None, ("role", "dom")),
            P(None, ("role", "dom")),
            P(None, ("role", "dom")),
            P(None, ("role", "dom")),
        ),
        check_vma=False,
    )
```

profile of v0, /device:TPU:1, one launch (start us, length us, event | category | flops | bytes accessed | tf_op | source)
XLA Modules:
  0.0 367.7 jit_solution(15414886028681906311)
XLA Ops:
  5.9 11.5 %all-to-all-start.1 = ((s32[128,1,2]{2,1,0:T(1,128)}), s32[128,1,2]{2,1,0:T(1,128)S(1)}, u32[]{:S(2)}, u32[]{:S(2)}) async-start(s32[128,1,2]{2,1,0:T(1,128)} %bitcast.25), calls=%async_computation.1 | async-start | bytes 131072 | tf_op jit(solution)/shard_map/all_to_all | solution.py:38
  19.6 3.7 collective-permute-start
  26.2 6.2 %scatter_fusion = f32[256,3,128]{2,1,0:T(4,128)S(1)} fusion(f32[256,3,128]{2,1,0:T(4,128)S(1)} %broadcast.217.clone, s32[192]{0:T(256)S(1)} %bitcast.213, f32[192,3,128]{2,1,0:T(4,128)S(1)} %gather_fusion), kind=kCustom, calls=%fused_computation.14 | custom fusion | bytes 885504 | tf_op jit(solution)/shard_map/scatter | solution.py:89
  33.5 9.5 %all-to-all-start = ((f32[128,2,3,128]{3,1,2,0:T(2,128)}), f32[128,2,3,128]{3,1,2,0:T(2,128)S(1)}, u32[]{:S(2)}, u32[]{:S(2)}) async-start(f32[128,2,3,128]{3,1,2,0:T(2,128)} %copy.81), calls=%async_computation | async-start | bytes 786432 | tf_op jit(solution)/shard_map/all_to_all | solution.py:37
  47.0 8.1 %all-to-all-done = f32[128,2,3,128]{3,1,2,0:T(2,128)S(1)} async-done(((f32[128,2,3,128]{3,1,2,0:T(2,128)}), f32[128,2,3,128]{3,1,2,0:T(2,128)S(1)}, u32[]{:S(2)}, u32[]{:S(2)}) %all-to-all-start) | async-done | bytes 393248 | tf_op jit(solution)/shard_map/all_to_all | solution.py:37
  55.4 67.4 %while.24 = (s32[]{:T(128)}, f32[8,32,3,128]{3,2,1,0:T(4,128)S(1)}, f32[8,32,3,128]{3,2,1,0:T(4,128)S(1)}, f32[8,32,3,128]{3,1,0,2:T(8,128)S(1)}, f32[8,32,3,128...) while((s32[]{:T(128)}, f32[8,32,3,128]{3,2,1,0:T(4,128)S(1)}, f32[8,32,3,128]{3,2,1,0:T(4,128)S(1)}, ...), condition=%wide.region_9.10_spmd, body=%wide.region_5.9_spmd.sunk | while | flops 47751200 | bytes 9210333 | solution.py:101
  55.5 2.1 multiply_reduce_fusion.12
  60.3 3.5 fusion.87
  63.9 2.1 multiply_reduce_fusion.12
  68.8 3.5 fusion.87
  72.3 2.1 multiply_reduce_fusion.12
  77.2 3.5 fusion.87
  80.8 2.1 multiply_reduce_fusion.12
  83.6 2.0 fusion.88
  85.6 3.5 fusion.87
  89.2 2.1 multiply_reduce_fusion.12
  92.0 2.0 fusion.88
  94.0 3.5 fusion.87
  97.6 2.1 multiply_reduce_fusion.12
  102.5 3.5 fusion.87
  106.0 2.1 multiply_reduce_fusion.12
  110.9 3.5 fusion.87
  114.5 2.1 multiply_reduce_fusion.12
  119.3 3.5 fusion.87
  123.8 4.8 %all-to-all-start.2 = ((f32[128,2,3,128]{3,1,2,0:T(2,128)}), f32[128,2,3,128]{3,1,2,0:T(2,128)S(1)}, u32[]{:S(2)}, u32[]{:S(2)}) async-start(f32[128,2,3,128]{3,1,2,0:T(2,128)} %copy.87), calls=%async_computation.2 | async-start | bytes 786432 | tf_op jit(solution)/shard_map/all_to_all | solution.py:43
  129.2 11.8 %all-to-all-done.2 = f32[128,2,3,128]{3,1,2,0:T(2,128)S(1)} async-done(((f32[128,2,3,128]{3,1,2,0:T(2,128)}), f32[128,2,3,128]{3,1,2,0:T(2,128)S(1)}, u32[]{:S(2)}, u32[]{:S(2)}) %all-to-all-start.2) | async-done | bytes 393248 | tf_op jit(solution)/shard_map/all_to_all | solution.py:43
  142.5 11.9 %fusion.63 = f32[96,3,128]{2,1,0:T(4,128)S(1)} fusion(f32[96,3,128]{2,1,0:T(4,128)S(1)} %bitcast_add_fusion.1, f32[96,128,128]{2,1,0:T(8,128)} %param.21), kind=kOutput, calls=%fused_computation.143 | convolution fusion | flops 56623104 | bytes 6586368 | tf_op jit(solution)/shard_map/bij,bcj->bci/dot_general | solution.py:126
  154.3 2.1 gather_fusion.3
  156.9 11.9 %fusion.37 = f32[96,3,128]{2,1,0:T(4,128)S(1)} fusion(f32[96,128,128]{2,1,0:T(8,128)} %param.21, f32[96,3,128]{2,1,0:T(4,128)S(1)} %bitcast_add_fusion.1, f32[96,3,128]{2,1,0:T(4,128)S(1)} %multiply_reduce_fusion.9), kind=kOutput, calls=%fused_computation.90 | convolution fusion | flops 56659968 | bytes 6733824 | tf_op jit(solution)/shard_map/bij,bcj->bci/dot_general | solution.py:129
  168.7 2.1 gather_fusion.4
  171.3 12.3 %fusion.35 = f32[96,3,128]{2,1,0:T(4,128)S(1)} fusion(f32[96,128,128]{2,1,0:T(8,128)} %param.21, f32[96,3,128]{2,1,0:T(4,128)S(1)} %bitcast_add_fusion.1, f32[96,3,128]{2,1,0:T(4,128)S(1)} %multiply_reduce_fusion.8), kind=kOutput, calls=%fused_computation.88 | convolution fusion | flops 56659968 | bytes 6733824 | tf_op jit(solution)/shard_map/bij,bcj->bci/dot_general | solution.py:129
  183.6 2.1 gather_fusion.5
  186.2 11.9 %fusion.33 = f32[96,3,128]{2,1,0:T(4,128)S(1)} fusion(f32[96,128,128]{2,1,0:T(8,128)} %param.21, f32[96,3,128]{2,1,0:T(4,128)S(1)} %bitcast_add_fusion.1, f32[96,3,128]{2,1,0:T(4,128)S(1)} %multiply_reduce_fusion.7), kind=kOutput, calls=%fused_computation.86 | convolution fusion | flops 56659968 | bytes 6733824 | tf_op jit(solution)/shard_map/bij,bcj->bci/dot_general | solution.py:129
  199.1 6.2 %scatter_fusion.1 = f32[256,3,128]{2,1,0:T(4,128)S(1)} fusion(f32[256,3,128]{2,1,0:T(4,128)S(1)} %broadcast.217, s32[192]{0:T(256)S(1)} %bitcast.214, f32[192,3,128]{2,1,0:T(4,128)S(1)} %gather_fusion.6), kind=kCustom, calls=%fused_computation.16 | custom fusion | bytes 885504 | tf_op jit(solution)/shard_map/scatter | solution.py:89
  206.3 4.5 %all-to-all-start.3 = ((f32[128,2,3,128]{3,1,2,0:T(2,128)}), f32[128,2,3,128]{3,1,2,0:T(2,128)S(1)}, u32[]{:S(2)}, u32[]{:S(2)}) async-start(f32[128,2,3,128]{3,1,2,0:T(2,128)} %copy.92), calls=%async_computation.3 | async-start | bytes 786432 | tf_op jit(solution)/shard_map/all_to_all | solution.py:37
  211.5 3.8 %collective-permute-start.1 = (f32[4,3,128]{2,1,0:T(4,128)S(1)}, f32[4,3,128]{2,1,0:T(4,128)S(1)}, u32[]{:S(2)}, u32[]{:S(2)}) collective-permute-start(f32[4,3,128]{2,1,0:T(4,128)S(1)} %gather_fusion.13), channel_id=1, source_target_pairs={{0,1},{1,2},{2,3},{3,4},{4,5},{5,6},{6,7},{7,8},{8,9},{9,10},{10,1... | collective-permute-start | bytes 18440 | tf_op jit(solution)/shard_map/ppermute | solution.py:21
  217.2 5.9 %all-to-all-done.3 = f32[128,2,3,128]{3,1,2,0:T(2,128)S(1)} async-done(((f32[128,2,3,128]{3,1,2,0:T(2,128)}), f32[128,2,3,128]{3,1,2,0:T(2,128)S(1)}, u32[]{:S(2)}, u32[]{:S(2)}) %all-to-all-start.3) | async-done | bytes 393248 | tf_op jit(solution)/shard_map/all_to_all | solution.py:37
  223.4 67.6 %while.25 = (s32[]{:T(128)}, f32[8,32,3,128]{3,2,1,0:T(4,128)S(1)}, f32[8,32,3,128]{3,2,1,0:T(4,128)S(1)}, f32[8,32,3,128]{3,1,0,2:T(8,128)S(1)}, f32[8,32,3,128...) while((s32[]{:T(128)}, f32[8,32,3,128]{3,2,1,0:T(4,128)S(1)}, f32[8,32,3,128]{3,2,1,0:T(4,128)S(1)}, ...), condition=%wide.region_21.22_spmd, body=%wide.region_17.21_spmd.sunk | while | flops 47751200 | bytes 9210333 | solution.py:101
  223.7 2.1 multiply_reduce_fusion.13
  226.5 2.0 fusion.92
  228.6 3.5 fusion.91
  232.1 2.1 multiply_reduce_fusion.13
  237.0 3.5 fusion.91
  240.6 2.1 multiply_reduce_fusion.13
  245.4 3.5 fusion.91
  249.0 2.1 multiply_reduce_fusion.13
  253.8 3.5 fusion.91
  257.4 2.1 multiply_reduce_fusion.13
  262.2 3.5 fusion.91
  265.8 2.1 multiply_reduce_fusion.13
  270.7 3.5 fusion.91
  274.3 2.1 multiply_reduce_fusion.13
  279.1 3.5 fusion.91
  282.7 2.1 multiply_reduce_fusion.13
  287.5 3.5 fusion.91
  292.5 5.0 %all-to-all-start.4 = ((f32[128,2,3,128]{3,1,2,0:T(2,128)}), f32[128,2,3,128]{3,1,2,0:T(2,128)S(1)}, u32[]{:S(2)}, u32[]{:S(2)}) async-start(f32[128,2,3,128]{3,1,2,0:T(2,128)} %copy.96), calls=%async_computation.4 | async-start | bytes 786432 | tf_op jit(solution)/shard_map/all_to_all | solution.py:43
  298.3 11.5 %all-to-all-done.4 = f32[128,2,3,128]{3,1,2,0:T(2,128)S(1)} async-done(((f32[128,2,3,128]{3,1,2,0:T(2,128)}), f32[128,2,3,128]{3,1,2,0:T(2,128)S(1)}, u32[]{:S(2)}, u32[]{:S(2)}) %all-to-all-start.4) | async-done | bytes 393248 | tf_op jit(solution)/shard_map/all_to_all | solution.py:43
  311.4 11.9 %fusion.64 = f32[96,3,128]{2,1,0:T(4,128)S(1)} fusion(f32[96,3,128]{2,1,0:T(4,128)S(1)} %multiply_add_fusion.1, f32[96,128,128]{2,1,0:T(8,128)} %param.21), kind=kOutput, calls=%fused_computation.144 | convolution fusion | flops 56623104 | bytes 6586368 | tf_op jit(solution)/shard_map/bij,bcj->bci/dot_general | solution.py:126
  323.2 2.1 gather_fusion.10
  325.8 11.9 %fusion.31 = f32[96,3,128]{2,1,0:T(4,128)S(1)} fusion(f32[96,128,128]{2,1,0:T(8,128)} %param.21, f32[96,3,128]{2,1,0:T(4,128)S(1)} %multiply_add_fusion.1, f32[96,3,128]{2,1,0:T(4,128)S(1)} %multiply_reduce_fusion.6), kind=kOutput, calls=%fused_computation.83 | convolution fusion | flops 56659968 | bytes 6733824 | tf_op jit(solution)/shard_map/bij,bcj->bci/dot_general | solution.py:129
  337.6 2.1 gather_fusion.11
  340.2 12.1 %fusion.29 = f32[96,3,128]{2,1,0:T(4,128)S(1)} fusion(f32[96,128,128]{2,1,0:T(8,128)} %param.21, f32[96,3,128]{2,1,0:T(4,128)S(1)} %multiply_add_fusion.1, f32[96,3,128]{2,1,0:T(4,128)S(1)} %multiply_reduce_fusion.5), kind=kOutput, calls=%fused_computation.81 | convolution fusion | flops 56659968 | bytes 6733824 | tf_op jit(solution)/shard_map/bij,bcj->bci/dot_general | solution.py:129
  352.3 2.1 gather_fusion.12
  354.9 12.6 %multiply_add_fusion = (f32[3,12288]{1,0:T(4,128)}, f32[3,12288]{1,0:T(4,128)}) fusion(f32[3,12288]{1,0:T(4,128)S(1)} %copy-done.1, f32[96,3,128]{2,1,0:T(4,128)S(1)} %fusion.33, f32[96,128,128]{2,1,0:T(8,128)} %param.21, f32[96,3,128]{2,1,0:T(4,128)S(1)} %multiply_add_fusion.1, f32[96,3,128]{2,1,0:T(4,128)S(1)} %multiply_reduce_fusion.4), kind=kOutput, calls=%fused_computation.79 | convolution fusion | flops 56807424 | bytes 7176192 | tf_op jit(solution)/shard_map/bij,bcj->bci/dot_general | solution.py:129
  (178 shorter events, 68.6 us)
Async XLA Ops:
  2.6 30.8 %copy-start.5 = (f32[96,3]{0,1:T(4,128)S(1)}, f32[96,3]{0,1:T(4,128)}, u32[]{:S(2)}) copy-start(f32[96,3]{0,1:T(4,128)} %param.23) | copy-start | bytes 3460
  5.9 27.5 %all-to-all-start.1 = ((s32[128,1,2]{2,1,0:T(1,128)}), s32[128,1,2]{2,1,0:T(1,128)S(1)}, u32[]{:S(2)}, u32[]{:S(2)}) async-start(s32[128,1,2]{2,1,0:T(1,128)} %bitcast.25), calls=%async_computation.1 | async-start | bytes 131072 | tf_op jit(solution)/shard_map/all_to_all | solution.py:38
  19.6 26.5 %collective-permute-start = (f32[4,3,128]{2,1,0:T(4,128)S(1)}, f32[4,3,128]{2,1,0:T(4,128)S(1)}, u32[]{:S(2)}, u32[]{:S(2)}) collective-permute-start(f32[4,3,128]{2,1,0:T(4,128)S(1)} %gather_fusion.7), channel_id=1, source_target_pairs={{0,1},{1,2},{2,3},{3,4},{4,5},{5,6},{6,7},{7,8},{8,9},{9,10},{10,1... | collective-permute-start | bytes 18440 | tf_op jit(solution)/shard_map/ppermute | solution.py:21
  26.1 18.7 %copy-start = (f32[3,8192]{1,0:T(4,128)S(1)}, f32[3,8192]{1,0:T(4,128)}, u32[]{:S(2)}) copy-start(f32[3,8192]{1,0:T(4,128)} %param.16) | copy-start | bytes 294916
  33.5 21.6 %all-to-all-start = ((f32[128,2,3,128]{3,1,2,0:T(2,128)}), f32[128,2,3,128]{3,1,2,0:T(2,128)S(1)}, u32[]{:S(2)}, u32[]{:S(2)}) async-start(f32[128,2,3,128]{3,1,2,0:T(2,128)} %copy.81), calls=%async_computation | async-start | bytes 786432 | tf_op jit(solution)/shard_map/all_to_all | solution.py:37
  122.8 6.1 %copy-start.4 = (s32[4]{0:T(128)S(1)}, s32[4]{0:T(128)}, u32[]{:S(2)}) copy-start(s32[4]{0:T(128)} %param.20) | copy-start | bytes 52
  123.8 17.2 %all-to-all-start.2 = ((f32[128,2,3,128]{3,1,2,0:T(2,128)}), f32[128,2,3,128]{3,1,2,0:T(2,128)S(1)}, u32[]{:S(2)}, u32[]{:S(2)}) async-start(f32[128,2,3,128]{3,1,2,0:T(2,128)} %copy.87), calls=%async_computation.2 | async-start | bytes 786432 | tf_op jit(solution)/shard_map/all_to_all | solution.py:43
  128.6 13.8 %copy-start.3 = (f32[3,12288]{1,0:T(4,128)S(1)}, f32[3,12288]{1,0:T(4,128)}, u32[]{:S(2)}) copy-start(f32[3,12288]{1,0:T(4,128)} %param.15) | copy-start | bytes 442372
  186.2 11.9 %copy-start.1 = (f32[3,12288]{1,0:T(4,128)S(1)}, f32[3,12288]{1,0:T(4,128)}, u32[]{:S(2)}) copy-start(f32[3,12288]{1,0:T(4,128)} %param.14) | copy-start | bytes 442372
  198.2 12.7 %copy-start.2 = (f32[3,8192]{1,0:T(4,128)S(1)}, f32[3,8192]{1,0:T(4,128)}, u32[]{:S(2)}) copy-start(f32[3,8192]{1,0:T(4,128)} %param.17) | copy-start | bytes 294916
  206.3 16.9 %all-to-all-start.3 = ((f32[128,2,3,128]{3,1,2,0:T(2,128)}), f32[128,2,3,128]{3,1,2,0:T(2,128)S(1)}, u32[]{:S(2)}, u32[]{:S(2)}) async-start(f32[128,2,3,128]{3,1,2,0:T(2,128)} %copy.92), calls=%async_computation.3 | async-start | bytes 786432 | tf_op jit(solution)/shard_map/all_to_all | solution.py:37
  211.5 4.8 %collective-permute-start.1 = (f32[4,3,128]{2,1,0:T(4,128)S(1)}, f32[4,3,128]{2,1,0:T(4,128)S(1)}, u32[]{:S(2)}, u32[]{:S(2)}) collective-permute-start(f32[4,3,128]{2,1,0:T(4,128)S(1)} %gather_fusion.13), channel_id=1, source_target_pairs={{0,1},{1,2},{2,3},{3,4},{4,5},{5,6},{6,7},{7,8},{8,9},{9,10},{10,1... | collective-permute-start | bytes 18440 | tf_op jit(solution)/shard_map/ppermute | solution.py:21
  292.5 17.3 %all-to-all-start.4 = ((f32[128,2,3,128]{3,1,2,0:T(2,128)}), f32[128,2,3,128]{3,1,2,0:T(2,128)S(1)}, u32[]{:S(2)}, u32[]{:S(2)}) async-start(f32[128,2,3,128]{3,1,2,0:T(2,128)} %copy.96), calls=%async_computation.4 | async-start | bytes 786432 | tf_op jit(solution)/shard_map/all_to_all | solution.py:43
where the time goes:
time: 372 us; the launch traced here: 368 us
  matrix products  186 us (50%)
  other arithmetic  53.4 us (14%)
  local copies, waits for them, and re-layouts  45.5 us (12%)
  starting transfers between devices  42.8 us (12%)
  waiting for transfers between devices  37.3 us (10%)
    dot_general x6, matrix products, local(): jnp.einsum('bij,bcj->bci', block_inverse, coupled, precision=lax.Precisio...  72.5 us
    dot_general x18, matrix products, pair_force(): jnp.einsum('nij,ncj->nci', weight, far_pos, precision=lax.Precision.HIGHEST)  57.1 us
    reduce_sum x18, other arithmetic, pair_force(): dist = jnp.sum(diff * diff, axis=1)  33.7 us
    dot_general x16, matrix products, pair_force(): jnp.einsum('nij,nci->ncj', weight, near_pos, precision=lax.Precision.HIGH...  32.2 us
    dot_general x2, matrix products, local(): jnp.einsum('bij,bcj->bci', block_inverse, rhs, precision=lax.Precision.HI...  23.7 us
    all_to_all x2, waiting for transfers between devices, inward(): lax.all_to_all(pushes, ('role', 'dom'), split_axis=0, concat_axis=0, tile...  23.3 us
    all_to_all x2, waiting for transfers between devices, outward(): lax.all_to_all(send_pos, ('role', 'dom'), split_axis=0, concat_axis=0, ti...  14 us
    all_to_all x2, starting transfers between devices, outward(): lax.all_to_all(send_pos, ('role', 'dom'), split_axis=0, concat_axis=0, ti...  14 us
  transfers between devices with their start and end apart: 7, of which 4 were waited for; matrix products, arithmetic and copies ran while one was open for 5% of the time, Pallas kernels for 0%

commit v1 on v0

v1 whole, which is shorter than its diff:
```python
import functools
import math

import jax
import jax.numpy as jnp
from jax import lax
from jax.experimental import pallas as pl
from jax.experimental.pallas import tpu as pltpu
from jax.sharding import PartitionSpec as P

BLK = 128
TOPC = 2
NNZB = 3
SWEEPS = 3
HB = 4
GROUP = 16
UNROLL = 8

BF = jnp.bfloat16
F32 = jnp.float32
MESH = pl.DeviceIdType.MESH

gain = 0.05
time_step = 0.1
spread_sq = 4.0
SCALE = math.sqrt(2.0 * math.log2(math.e) / spread_sq)


def split2(x):
    hi = x.astype(BF).astype(F32)
    return hi, x - hi


def split3(x):
    hi = x.astype(BF).astype(F32)
    rest = x - hi
    mid = rest.astype(BF).astype(F32)
    return hi, mid, rest - mid


def dot(a, b):
    return jnp.dot(a, b, preferred_element_type=F32)


def dot_nt(a, b):
    return lax.dot_general(a, b, (((1,), (1,)), ((), ())), preferred_element_type=F32)


def dot_tn(a, b):
    return lax.dot_general(a, b, (((0,), (0,)), ((), ())), preferred_element_type=F32)


def pair(near, far):
    row = lax.broadcasted_iota(jnp.int32, (8, BLK), 0)
    near_s = near * SCALE
    far_s = far * SCALE

    def norms(t):
        sq = t * t * (-0.5)
        first = jnp.sum(jnp.where(row < 3, sq, 0.0), axis=0, keepdims=True)
        second = jnp.sum(
            jnp.where((row >= 3) & (row < 6), sq, 0.0), axis=0, keepdims=True
        )
        return first, second

    nx0, nx1 = norms(near_s)
    ny = norms(far_s)
    xh, xm, xl = split3(jnp.where(row < 6, near_s, jnp.where(row == 6, nx0, nx1)))
    one = jnp.ones((8, BLK), F32)
    lhs = jnp.concatenate([xh, xm, xl, xh, xm, xh, one, one], axis=0).astype(BF)
    yh, ym, yl = split3(jnp.where(row < 6, far_s, 0.0))
    sides = []
    for k in range(2):
        mask = (row >= 3 * k) & (row < 3 * k + 3)

        def keep(t):
            return jnp.where(mask, t, 0.0)

        yhk = keep(yh) + (row == 6 + k).astype(F32)
        nh, nm, nl = split3(ny[k])
        nrows = jnp.where(
            row == 0, nh, jnp.where(row == 1, nm, jnp.where(row == 2, nl, 0.0))
        )
        sides.append(
            jnp.concatenate(
                [yhk, yhk, yhk, keep(ym), keep(ym), keep(yl), nrows, one * 0.0], axis=0
            )
        )
    rhs = jnp.concatenate(sides, axis=1).astype(BF)
    weight = jnp.exp2(jnp.minimum(dot_tn(lhs, rhs), 0.0))
    w_hi = weight.astype(BF)
    w_lo = (weight - w_hi.astype(F32)).astype(BF)
    h0, h1 = w_hi[:, :BLK], w_hi[:, BLK:]
    l0, l1 = w_lo[:, :BLK], w_lo[:, BLK:]

    def features(t):
        h, l = split2(t)
        h = jnp.where(row == 6, 1.0, jnp.where(row == 7, 0.0, h))
        l = jnp.where(row < 6, l, 0.0)
        a = jnp.concatenate([h, l], axis=0).astype(BF)
        return jnp.concatenate([a, a], axis=1)

    over_near = jnp.concatenate([w_hi, w_lo], axis=0)
    over_far = jnp.concatenate(
        [jnp.concatenate([h0, l0], axis=1), jnp.concatenate([h1, l1], axis=1)], axis=0
    )
    sum_near = dot(features(near), over_near)
    sum_far = dot_nt(features(far), over_far)

    def force(t, o):
        a = o[0:8, :BLK] + o[8:16, :BLK]
        b = o[0:8, BLK:] + o[8:16, BLK:]
        total = jnp.where(row < 3, a[6:7, :], b[6:7, :])
        return gain * (t * total - jnp.where(row < 3, a, b))

    return force(near, sum_far), force(far, sum_near)


def kernel(
    n,
    n_dom,
    nb,
    nt,
    tire_pos,
    tire_vel,
    part_pos,
    part_vel,
    owner,
    ctile,
    halo,
    binv,
    pattern,
    coup,
    o_tp,
    o_tv,
    o_pp,
    o_pv,
    bstage,
    bsplit,
    nscr,
    pscr,
    send1,
    near1,
    far1,
    push1,
    pret,
    react1,
    tsend,
    tret,
    near2,
    push2,
    react2,
    rret,
    edge,
    hrecv,
    hpush,
    vs,
    vo,
    tst,
    sk_t,
    sk_n,
    oh_n,
    oh_t,
    bsem,
    ssem,
    rsem1,
    psem,
    tsem,
    rrsem,
    hsem,
    hssem,
):
    me = lax.axis_index("role") * n_dom + lax.axis_index("dom")

    def dev(p):
        return (p // n_dom, p % n_dom)

    def ahead(i):
        return dev((me + i) % n)

    def behind(i):
        return dev((me + n - i) % n)

    barrier = pltpu.get_barrier_semaphore()

    def greet(i, c):
        pl.semaphore_signal(barrier, inc=1, device_id=ahead(i), device_id_type=MESH)
        return c

    lax.fori_loop(1, n, greet, 0)

    bcopy = pltpu.make_async_copy(binv, bstage, bsem)
    bcopy.start()

    def tile_rows(i, rows=8):
        return pl.ds(pl.multiple_of(i * 8, 8), rows)

    def comps(ref, count, first=0):
        return [ref[pl.ds(first + c, count, stride=8), :] for c in range(3)]

    def put(ref, count, vals, first=0):
        for c in range(len(vals)):
            ref[pl.ds(first + c, count, stride=8), :] = vals[c]

    def spread(src, scr, count):
        for b in range(count):
            scr[b * 8 : b * 8 + 3, :] = src[:, b * BLK : (b + 1) * BLK]

    def collect(scr, dst, count):
        for b in range(count):
            dst[:, b * BLK : (b + 1) * BLK] = scr[b * 8 : b * 8 + 3, :]

    lane = lax.broadcasted_iota(jnp.int32, (BLK, BLK), 1)
    sub = lax.broadcasted_iota(jnp.int32, (BLK, BLK), 0)

    def pad_rows(x, rows=BLK):
        if x.shape[0] == rows:
            return x
        return jnp.concatenate(
            [x, jnp.zeros((rows - x.shape[0], x.shape[1]), x.dtype)], axis=0
        )

    lane_b = lax.broadcasted_iota(jnp.int32, (nb, BLK), 1)
    hot = jnp.zeros((nb, BLK), F32)
    tile_of = jnp.zeros((nb, BLK), F32)
    for m in range(TOPC):
        rel = (owner[:, m : m + 1] - me + n) & (n - 1)
        is_m = lane_b == rel
        hot = hot + jnp.where(is_m, 1.0, 0.0)
        tile_of = tile_of + jnp.where(
            is_m, (ctile[:, m : m + 1] + 1).astype(F32), 0.0
        )
    hot_p = pad_rows(hot)
    lower = jnp.where(lane < sub, 1.0, 0.0).astype(BF)
    rank = dot(lower, hot_p.astype(BF))
    tile_p = pad_rows(tile_of)
    ids = []
    for k in range(2):
        u = jnp.where((hot_p > 0.5) & (jnp.abs(rank - k) < 0.5), tile_p, 0.0)
        ut = jnp.transpose(u)
        sk_t[k] = jnp.where(u > 0.5, 1.0, 0.0).astype(BF)
        sk_n[k] = jnp.where(ut > 0.5, 1.0, 0.0).astype(BF)
        ids.append(jnp.sum(ut, axis=1, keepdims=True) - 1.0)

    def node_slots(x, dst):
        cat = jnp.concatenate(x, axis=1)
        parts = [pad_rows(t.astype(BF)) for t in split3(cat)]
        for k in range(2):
            g = dot(sk_n[k], parts[0]) + dot(sk_n[k], parts[1]) + dot(sk_n[k], parts[2])
            put(dst, n, [g[:, c * BLK : (c + 1) * BLK] for c in range(3)], 3 * k)

    spread(tire_pos, nscr, nb)
    tp = comps(nscr, nb)
    node_slots(tp, send1)
    send1[pl.ds(6, n, stride=8), :] = jnp.where(
        lane < nt, jnp.broadcast_to(ids[0], (n, BLK)), jnp.broadcast_to(ids[1], (n, BLK))
    )

    pl.semaphore_wait(barrier, n - 1)

    def wait_rows(ref, sem, count, rows):
        view = ref.at[pl.ds(0, count * rows), :]
        pltpu.make_async_copy(view, view, sem).wait()

    def remote(src, dst, i, rows, sem_s, sem_r, target):
        pltpu.make_async_remote_copy(
            src_ref=src.at[tile_rows(i, rows), :],
            dst_ref=dst.at[tile_rows(i, rows), :],
            send_sem=sem_s,
            recv_sem=sem_r,
            device_id=target,
            device_id_type=MESH,
        ).start()

    def own(src, dst, rows, sem_r):
        pltpu.make_async_copy(
            src.at[pl.ds(0, rows), :], dst.at[pl.ds(0, rows), :], sem_r
        ).start()

    own(send1, near1, 7, rsem1.at[0])

    def send_pos(i, c):
        remote(send1, near1, i, 7, ssem.at[0], rsem1.at[i // GROUP], ahead(i))
        return c

    lax.fori_loop(1, n, send_pos, 0)

    def tiles_split(x):
        cat = jnp.concatenate(x, axis=1)
        for s, t in enumerate(split3(cat)):
            t = t.astype(BF)
            tst[s, 0:nt, :] = t
            tst[s, nt : 2 * nt, :] = t

    def send_edges(step):
        for u in range(2):
            a = pscr[pl.ds(halo[2 * u] * 8, 8), :]
            b = pscr[pl.ds(halo[2 * u + 1] * 8, 8), :]
            edge[pl.ds((2 * step + u) * 8, 8), :] = jnp.concatenate(
                [a[0:3], b[0:3], jnp.zeros((2, BLK), F32)], axis=0
            )
        pltpu.make_async_remote_copy(
            src_ref=edge.at[pl.ds(step * 16, 16), :],
            dst_ref=hrecv.at[pl.ds(step * 16, 16), :],
            send_sem=hssem.at[step],
            recv_sem=hsem.at[step],
            device_id=ahead(1),
            device_id_type=MESH,
        ).start()

    spread(part_pos, pscr, nt)
    pp = comps(pscr, nt)
    tiles_split(pp)
    send_edges(0)

    live = jnp.where(me > 0, 1.0, 0.0).astype(F32)
    sub_t = lax.broadcasted_iota(jnp.int32, (nt, BLK), 0)

    def halo_force(step):
        view = hrecv.at[pl.ds(step * 16, 16), :]
        pltpu.make_async_copy(view, view, hsem.at[step]).wait()
        out = [jnp.zeros((nt, BLK), F32) for _ in range(3)]
        for u in range(2):
            at = pl.ds((2 * step + u) * 8, 8)
            force, unused = pair(edge[at, :], hrecv[at, :])
            force = force * live
            for k in range(2):
                here = sub_t == halo[2 * u + k]
                for c in range(3):
                    r = 3 * k + c
                    out[c] = out[c] + jnp.where(here, force[r : r + 1, :], 0.0)
        return out

    bcopy.wait()

    def split_block(q, c):
        for s in range(2):
            b = bstage[2 * q + s]
            hi = b.astype(BF)
            bsplit[q, s * BLK : (s + 1) * BLK, 0:BLK] = hi
            bsplit[q, s * BLK : (s + 1) * BLK, BLK : 2 * BLK] = (
                b - hi.astype(F32)
            ).astype(BF)
        return c

    lax.fori_loop(0, nb // 2, split_block, 0)

    cmat = jnp.zeros((nb, BLK), F32)
    for m in range(NNZB):
        cmat = cmat + jnp.where(lane_b == pattern[:, m : m + 1], coup[:, m : m + 1], 0.0)
    c_hi = cmat.astype(BF)
    c_lo = (cmat - c_hi.astype(F32)).astype(BF)
    vs[...] = jnp.zeros_like(vs)

    def matvec(x):
        for c in range(3):
            h, l = split2(x[c])
            vs[pl.ds(c, nb, stride=8), :] = h
            vs[pl.ds(3 + c, nb, stride=8), :] = l

        def some(j, carry):
            for u in range(UNROLL):
                q = j * UNROLL + u
                at = pl.ds(pl.multiple_of(q * 16, 16), 16)
                t = vs[at, :].astype(BF)
                o = dot_nt(jnp.concatenate([t, t], axis=1), bsplit[q])
                vo[at, :] = jnp.concatenate([o[0:8, :BLK], o[8:16, BLK:]], axis=0)
            return carry

        lax.fori_loop(0, nb // 2 // UNROLL, some, 0)
        a, b = comps(vo, nb), comps(vo, nb, 3)
        return [a[c] + b[c] for c in range(3)]

    def couple(v):
        h, l = split2(jnp.concatenate(v, axis=1))
        h, l = pad_rows(h.astype(BF)), pad_rows(l.astype(BF))
        o = dot(c_hi, h) + dot(c_lo, h) + dot(c_hi, l)
        return [o[:, c * BLK : (c + 1) * BLK] for c in range(3)]

    def solve(rhs):
        v = matvec(rhs)
        for _ in range(SWEEPS):
            w = couple(v)
            v = matvec([rhs[c] + w[c] for c in range(3)])
        return v

    def by_slot(ref, k):
        return jnp.concatenate(comps(ref, n, 3 * k), axis=1)

    def gather_sum(mats, ref):
        total = None
        for k in range(2):
            h, l = split2(by_slot(ref, k))
            o = dot(mats[k], h.astype(BF)) + dot(mats[k], l.astype(BF))
            total = o if total is None else total + o
        return [total[:, c * BLK : (c + 1) * BLK] for c in range(3)]

    def soil_sum(ref):
        return gather_sum([oh_t[0:nt, :], oh_t[nt : 2 * nt, :]], ref)

    def node_sum(ref):
        return gather_sum([sk_t[0, 0:nb, :], sk_t[1, 0:nb, :]], ref)

    lane_g = lax.broadcasted_iota(jnp.int32, (GROUP, BLK), 1)
    lane_gm = (lane_g & (nt - 1)).astype(F32)

    def owner_group(g, c):
        base = pl.multiple_of(g * GROUP * 8, GROUP * 8)
        wait_rows(near1, rsem1.at[g], GROUP, 7)
        tid = near1[pl.ds(base + 6, GROUP, stride=8), :]
        oh = jnp.where(tid == lane_gm, 1.0, 0.0)
        sel = jnp.concatenate(
            [jnp.where(lane_g < nt, oh, 0.0), jnp.where(lane_g < nt, 0.0, oh)], axis=0
        ).astype(BF)
        got = dot(sel, tst[0]) + dot(sel, tst[1]) + dot(sel, tst[2])
        for k in range(2):
            for cc in range(3):
                far1[pl.ds(base + 3 * k + cc, GROUP, stride=8), :] = got[
                    k * GROUP : (k + 1) * GROUP, cc * BLK : (cc + 1) * BLK
                ]

        def some(j, carry):
            for u in range(UNROLL):
                i = g * GROUP + j * UNROLL + u
                at = tile_rows(i)
                push1[at, :], react1[at, :] = pair(near1[at, :], far1[at, :])
            for u in range(UNROLL):
                i = g * GROUP + j * UNROLL + u

                @pl.when(i > 0)
                def _():
                    remote(push1, pret, i, 6, ssem.at[1], psem, behind(i))

                @pl.when(i == 0)
                def _():
                    own(push1, pret, 6, psem)

            return carry

        lax.fori_loop(0, GROUP // UNROLL, some, 0)
        return c

    lax.fori_loop(0, n // GROUP, owner_group, 0)

    lane_m = (lane & (nt - 1)).astype(F32)
    oh_all = jnp.where(near1[pl.ds(6, n, stride=8), :] == lane_m, 1.0, 0.0)
    oh_n[0] = jnp.where(lane < nt, oh_all, 0.0).astype(BF)
    oh_n[1] = jnp.where(lane < nt, 0.0, oh_all).astype(BF)
    oh_t[...] = jnp.transpose(oh_all).astype(BF)

    hf = halo_force(0)
    sf = soil_sum(react1)
    spread(part_vel, pscr, nt)
    pv = comps(pscr, nt)
    pv = [pv[c] + time_step * (sf[c] + hf[c]) for c in range(3)]
    pp = [pp[c] + time_step * pv[c] for c in range(3)]
    put(pscr, nt, pp)
    tiles_split(pp)
    for k in range(2):
        got = dot(oh_n[k], tst[0]) + dot(oh_n[k], tst[1]) + dot(oh_n[k], tst[2])
        put(tsend, n, [got[:, c * BLK : (c + 1) * BLK] for c in range(3)], 3 * k)

    own(tsend, tret, 6, tsem.at[0])

    def send_tiles(i, c):
        remote(tsend, tret, i, 6, ssem.at[2], tsem.at[i // GROUP], behind(i))
        return c

    lax.fori_loop(1, n, send_tiles, 0)
    send_edges(1)

    spread(tire_vel, nscr, nb)
    tv = comps(nscr, nb)
    wait_rows(pret, psem, n, 6)
    nf = node_sum(pret)
    tv = solve([tv[c] + time_step * nf[c] for c in range(3)])
    tp = [tp[c] + time_step * tv[c] for c in range(3)]
    node_slots(tp, near2)

    def node_group(g, c):
        wait_rows(tret, tsem.at[g], GROUP, 6)

        def some(j, carry):
            for u in range(UNROLL):
                i = g * GROUP + j * UNROLL + u
                at = tile_rows(i)
                push2[at, :], react2[at, :] = pair(near2[at, :], tret[at, :])
            for u in range(UNROLL):
                i = g * GROUP + j * UNROLL + u

                @pl.when(i > 0)
                def _():
                    remote(react2, rret, i, 6, ssem.at[3], rrsem, ahead(i))

                @pl.when(i == 0)
                def _():
                    own(react2, rret, 6, rrsem)

            return carry

        lax.fori_loop(0, GROUP // UNROLL, some, 0)
        return c

    lax.fori_loop(0, n // GROUP, node_group, 0)

    nf = node_sum(push2)
    tv = solve([tv[c] + time_step * nf[c] for c in range(3)])
    tp = [tp[c] + time_step * tv[c] for c in range(3)]
    put(nscr, nb, tv)
    collect(nscr, o_tv, nb)
    put(nscr, nb, tp)
    collect(nscr, o_tp, nb)

    hf = halo_force(1)
    wait_rows(rret, rrsem, n, 6)
    sf = soil_sum(rret)
    pv = [pv[c] + time_step * (sf[c] + hf[c]) for c in range(3)]
    pp = [pp[c] + time_step * pv[c] for c in range(3)]
    put(pscr, nt, pv)
    collect(pscr, o_pv, nt)
    put(pscr, nt, pp)
    collect(pscr, o_pp, nt)

    wait_rows(send1, ssem.at[0], n - 1, 7)
    for s in range(1, 4):
        wait_rows(push1, ssem.at[s], n - 1, 6)
    for step in range(2):
        view = edge.at[pl.ds(step * 16, 16), :]
        pltpu.make_async_copy(view, view, hssem.at[step]).wait()


def local(
    n,
    n_dom,
    tire_pos,
    tire_vel,
    part_pos,
    part_vel,
    contact_owner,
    contact_tile,
    halo_tiles,
    block_inverse,
    pattern,
    coupling,
):
    nb = tire_pos.shape[1] // BLK
    nt = part_pos.shape[1] // BLK
    vmem = pl.BlockSpec(memory_space=pltpu.VMEM)
    smem = pl.BlockSpec(memory_space=pltpu.SMEM)
    hbm = pl.BlockSpec(memory_space=pl.ANY)
    message = pltpu.VMEM((n * 8, BLK), F32)
    return pl.pallas_call(
        functools.partial(kernel, n, n_dom, nb, nt),
        out_shape=(
            jax.ShapeDtypeStruct(tire_pos.shape, F32),
            jax.ShapeDtypeStruct(tire_pos.shape, F32),
            jax.ShapeDtypeStruct(part_pos.shape, F32),
            jax.ShapeDtypeStruct(part_pos.shape, F32),
        ),
        in_specs=[vmem, vmem, vmem, vmem, vmem, vmem, smem, hbm, vmem, vmem],
        out_specs=[vmem] * 4,
        scratch_shapes=[
            pltpu.VMEM((nb, BLK, BLK), F32),
            pltpu.VMEM((nb // 2, 2 * BLK, 2 * BLK), BF),
            pltpu.VMEM((nb * 8, BLK), F32),
            pltpu.VMEM((nt * 8, BLK), F32),
        ]
        + [message] * 12
        + [
            pltpu.VMEM((32, BLK), F32),
            pltpu.VMEM((32, BLK), F32),
            pltpu.VMEM((16, BLK), F32),
            pltpu.VMEM((nb * 8, BLK), F32),
            pltpu.VMEM((nb * 8, BLK), F32),
            pltpu.VMEM((3, 2 * nt, 3 * BLK), BF),
            pltpu.VMEM((2, BLK, BLK), BF),
            pltpu.VMEM((2, BLK, BLK), BF),
            pltpu.VMEM((2, BLK, BLK), BF),
            pltpu.VMEM((BLK, BLK), BF),
            pltpu.SemaphoreType.DMA,
            pltpu.SemaphoreType.DMA((4,)),
            pltpu.SemaphoreType.DMA((n // GROUP,)),
            pltpu.SemaphoreType.DMA,
            pltpu.SemaphoreType.DMA((n // GROUP,)),
            pltpu.SemaphoreType.DMA,
            pltpu.SemaphoreType.DMA((2,)),
            pltpu.SemaphoreType.DMA((2,)),
        ],
        compiler_params=pltpu.CompilerParams(
            collective_id=0, has_side_effects=True, vmem_limit_bytes=48 << 20
        ),
    )(
        tire_pos,
        tire_vel,
        part_pos,
        part_vel,
        contact_owner,
        contact_tile,
        halo_tiles,
        block_inverse,
        pattern,
        coupling,
    )


def solution(mesh):
    n_role, n_dom = mesh.shape["role"], mesh.shape["dom"]
    both = ("role", "dom")
    return jax.shard_map(
        functools.partial(local, n_role * n_dom, n_dom),
        mesh=mesh,
        in_specs=(
            P(None, both),
            P(None, both),
            P(None, both),
            P(None, both),
            P(both, None),
            P(both, None),
            P(both),
            P(both, None, None),
            P(both, None),
            P(both, None),
        ),
        out_specs=(P(None, both), P(None, both), P(None, both), P(None, both)),
        check_vma=False,
    )
```

time: 372 us -> 103 us (0.28); the launches traced: 368 us -> 103 us
  matrix products: 186 us -> 0 us
  Pallas kernels: 0 us -> 92.1 us
  other arithmetic: 53.4 us -> 0 us
  starting transfers between devices: 42.8 us -> 0 us
  waiting for transfers between devices: 37.3 us -> 0 us
  local copies, waits for them, and re-layouts: 45.5 us -> 10.1 us
    dot_general x46 -> x0, matrix products: 186 us -> none  [the longest x6 72.5 us: local(): jnp.einsum('bij,bcj->bci', block_inverse, coupled, precision=lax.Precisio...]
    pallas_call x0 -> x1, Pallas kernels: none -> 92.1 us  [local(): pl.pallas_call(functools.partial(kernel, n, n_dom, nb, nt), out_shape=(ja...]
    reduce_sum x45 -> x0, other arithmetic: 48.6 us -> none  [the longest x18 33.7 us: pair_force(): dist = jnp.sum(diff * diff, axis=1)]
    all_to_all x5 -> x0, waiting for transfers between devices: 37.3 us -> none  [the longest x2 23.3 us: inward(): lax.all_to_all(pushes, ('role', 'dom'), split_axis=0, concat_axis=0, tile...]
    all_to_all x5 -> x0, starting transfers between devices: 35.3 us -> none  [the longest x2 14 us: outward(): lax.all_to_all(send_pos, ('role', 'dom'), split_axis=0, concat_axis=0, ti...]
    gather x14 -> x0, local copies, waits for them, and re-layouts: 21.4 us -> none  [the longest x6 12.9 us: local(): velocity[pattern]]
    scatter x3 -> x0, local copies, waits for them, and re-layouts: 13.6 us -> none  [the longest x2 12.4 us: local(): jnp.zeros((slot_total, 3, BLK), jnp.float32).at[dest_slot]]
    unnamed x16 -> x18, local copies, waits for them, and re-layouts: 1.7 us -> 10.1 us
  transfers between devices with their start and end apart: 7 -> 0, of which waited for: 4 -> 0; matrix products, arithmetic and copies ran while one was open for 5% -> 0% of each run, Pallas kernels for 0% -> 0%
where the time goes in v1:
time: 103 us
  Pallas kernels  92.1 us (89%)
  local copies, waits for them, and re-layouts  10.1 us (10%)
    pallas_call x1, Pallas kernels, local(): pl.pallas_call(functools.partial(kernel, n, n_dom, nb, nt), out_shape=(ja...  92.1 us
    unnamed x18, local copies, waits for them, and re-layouts  10.1 us

profile of v1, /device:TPU:1, one launch (start us, length us, event | category | flops | bytes accessed | tf_op | source)
XLA Modules:
  0.0 102.9 jit_solution(13600719280690672332)
XLA Ops:
  0.6 0.8 copy.14.owner
  1.4 0.8 copy.15.ctile
  2.2 0.8 copy.16.pattern
  3.0 0.8 copy.17.coup
  3.7 0.0 copy-start
  3.7 0.9 copy-done
  4.7 0.0 copy-start.1
  4.7 0.9 copy-done.1
  5.6 0.0 copy-start.2
  5.6 0.9 copy-done.2
  6.5 0.0 copy-start.3
  6.5 0.9 copy-done.3
  7.4 0.0 copy-start.4
  7.4 0.7 copy-done.4
  8.1 92.1 %shard_map.129 = (f32[3,12288]{1,0:T(4,128)S(1)}, f32[3,12288]{1,0:T(4,128)S(1)}, f32[3,8192]{1,0:T(4,128)S(1)}, f32[3,8192]{1,0:T(4,128)S(1)}) custom-call(f32[3,12288]{1,0:T(4,128)S(1)} %copy-done, f32[3,12288]{1,0:T(4,128)S(1)} %copy-done.1, f32[3,8192]{1,0:T(4,128)S(1)} %copy-done.2, f32[3,8192]{1,0:T(4,128)S(1)} %copy-done.3, s32[96,2]{1,0:T(8,128)S(1)} %copy.14.owner, ...), custom_call_target="tpu_custom_call" | custom-call | tf_op jit(solution)/shard_map/pallas_call | solution.py:552
  100.2 0.7 copy.22
  100.9 0.7 copy.23
  101.6 0.7 copy.24
  102.2 0.7 copy.25
Async XLA Ops:
  3.7 0.9 copy-start
  4.7 0.9 copy-start.1
  5.6 0.9 copy-start.2
  6.5 0.9 copy-start.3
  7.4 0.7 copy-start.4

commit v2 on v1

--- a/solution.py
+++ b/solution.py
@@ -14,7 +14,7 @@
 SWEEPS = 3
 HB = 4
 GROUP = 16
-UNROLL = 8
+UNROLL = 16
 
 BF = jnp.bfloat16
 F32 = jnp.float32
@@ -50,7 +50,7 @@
     return lax.dot_general(a, b, (((0,), (0,)), ((), ())), preferred_element_type=F32)
 
 
-def pair(near, far):
+def pair_weights(near, far):
     row = lax.broadcasted_iota(jnp.int32, (8, BLK), 0)
     near_s = near * SCALE
     far_s = far * SCALE
@@ -89,31 +89,40 @@
     rhs = jnp.concatenate(sides, axis=1).astype(BF)
     weight = jnp.exp2(jnp.minimum(dot_tn(lhs, rhs), 0.0))
     w_hi = weight.astype(BF)
-    w_lo = (weight - w_hi.astype(F32)).astype(BF)
-    h0, h1 = w_hi[:, :BLK], w_hi[:, BLK:]
-    l0, l1 = w_lo[:, :BLK], w_lo[:, BLK:]
-
-    def features(t):
-        h, l = split2(t)
-        h = jnp.where(row == 6, 1.0, jnp.where(row == 7, 0.0, h))
-        l = jnp.where(row < 6, l, 0.0)
-        a = jnp.concatenate([h, l], axis=0).astype(BF)
-        return jnp.concatenate([a, a], axis=1)
-
-    over_near = jnp.concatenate([w_hi, w_lo], axis=0)
-    over_far = jnp.concatenate(
-        [jnp.concatenate([h0, l0], axis=1), jnp.concatenate([h1, l1], axis=1)], axis=0
-    )
-    sum_near = dot(features(near), over_near)
-    sum_far = dot_nt(features(far), over_far)
-
-    def force(t, o):
-        a = o[0:8, :BLK] + o[8:16, :BLK]
-        b = o[0:8, BLK:] + o[8:16, BLK:]
-        total = jnp.where(row < 3, a[6:7, :], b[6:7, :])
-        return gain * (t * total - jnp.where(row < 3, a, b))
-
-    return force(near, sum_far), force(far, sum_near)
+    return w_hi, (weight - w_hi.astype(F32)).astype(BF)
+
+
+def features(t):
+    row = lax.broadcasted_iota(jnp.int32, (8, BLK), 0)
+    h, l = split2(t)
+    h = jnp.where(row == 6, 1.0, jnp.where(row == 7, 0.0, h))
+    l = jnp.where(row < 6, l, 0.0)
+    return jnp.concatenate([h, l], axis=0).astype(BF)
+
+
+def force(t, a, b):
+    row = lax.broadcasted_iota(jnp.int32, (8, BLK), 0)
+    a = a[0:8] + a[8:16]
+    b = b[0:8] + b[8:16]
+    total = jnp.where(row < 3, a[6:7, :], b[6:7, :])
+    return gain * (t * total - jnp.where(row < 3, a, b))
+
+
+def put_weights(ws, u, near, far):
+    ws[u, 0:BLK, :], ws[u, BLK : 2 * BLK, :] = pair_weights(near, far)
+
+
+def react_of(ws, u, near, far):
+    f = features(near)
+    o = dot(jnp.concatenate([f, f], axis=1), ws[u])
+    return force(far, o[:, :BLK], o[:, BLK:])
+
+
+def push_of(ws, u, near, far):
+    f = features(far)
+    a = dot_nt(f, ws[u, :, :BLK])
+    b = dot_nt(f, ws[u, :, BLK:])
+    return force(near, a[:, :BLK] + a[:, BLK:], b[:, :BLK] + b[:, BLK:])
 
 
 def kernel(
@@ -135,6 +144,16 @@
     o_tv,
     o_pp,
     o_pv,
+    s_tp,
+    s_tv,
+    s_pp,
+    s_pv,
+    s_owner,
+    s_ctile,
+    s_halo,
+    s_pattern,
+    s_coup,
+    ws,
     bstage,
     bsplit,
     nscr,
@@ -161,6 +180,7 @@
     sk_n,
     oh_n,
     oh_t,
+    insem,
     bsem,
     ssem,
     rsem1,
@@ -181,6 +201,27 @@
     def behind(i):
         return dev((me + n - i) % n)
 
+    arrive = []
+    for k, (src, dst) in enumerate(
+        [
+            (tire_pos, s_tp),
+            (owner, s_owner),
+            (ctile, s_ctile),
+            (part_pos, s_pp),
+            (halo, s_halo),
+            (part_vel, s_pv),
+            (tire_vel, s_tv),
+            (pattern, s_pattern),
+            (coup, s_coup),
+        ]
+    ):
+        arrive.append(pltpu.make_async_copy(src, dst, insem.at[k]))
+        arrive[k].start()
+
+    def ready(first, last):
+        for k in range(first, last):
+            arrive[k].wait()
+
     barrier = pltpu.get_barrier_semaphore()
 
     def greet(i, c):
@@ -220,27 +261,30 @@
             [x, jnp.zeros((rows - x.shape[0], x.shape[1]), x.dtype)], axis=0
         )
 
-    lane_b = lax.broadcasted_iota(jnp.int32, (nb, BLK), 1)
-    hot = jnp.zeros((nb, BLK), F32)
-    tile_of = jnp.zeros((nb, BLK), F32)
+    ready(0, 3)
+    sub_b = lax.broadcasted_iota(jnp.int32, (BLK, nb), 0)
+    hot = jnp.zeros((BLK, nb), F32)
+    tile_of = jnp.zeros((BLK, nb), F32)
     for m in range(TOPC):
-        rel = (owner[:, m : m + 1] - me + n) & (n - 1)
-        is_m = lane_b == rel
+        rel = (s_owner[m : m + 1, :] - me + n) & (n - 1)
+        is_m = sub_b == rel
         hot = hot + jnp.where(is_m, 1.0, 0.0)
         tile_of = tile_of + jnp.where(
-            is_m, (ctile[:, m : m + 1] + 1).astype(F32), 0.0
+            is_m, (s_ctile[m : m + 1, :] + 1).astype(F32), 0.0
         )
-    hot_p = pad_rows(hot)
-    lower = jnp.where(lane < sub, 1.0, 0.0).astype(BF)
-    rank = dot(lower, hot_p.astype(BF))
-    tile_p = pad_rows(tile_of)
+
+    def pad_lanes(x):
+        return jnp.concatenate([x, jnp.zeros((BLK, BLK - nb), x.dtype)], axis=1)
+
+    hot_p = pad_lanes(hot)
+    upper = jnp.where(sub < lane, 1.0, 0.0).astype(BF)
+    rank = dot(hot_p.astype(BF), upper)
+    tile_p = pad_lanes(tile_of)
     ids = []
     for k in range(2):
         u = jnp.where((hot_p > 0.5) & (jnp.abs(rank - k) < 0.5), tile_p, 0.0)
-        ut = jnp.transpose(u)
-        sk_t[k] = jnp.where(u > 0.5, 1.0, 0.0).astype(BF)
-        sk_n[k] = jnp.where(ut > 0.5, 1.0, 0.0).astype(BF)
-        ids.append(jnp.sum(ut, axis=1, keepdims=True) - 1.0)
+        sk_n[k] = jnp.where(u > 0.5, 1.0, 0.0).astype(BF)
+        ids.append(jnp.sum(u, axis=1, keepdims=True) - 1.0)
 
     def node_slots(x, dst):
         cat = jnp.concatenate(x, axis=1)
@@ -249,7 +293,7 @@
             g = dot(sk_n[k], parts[0]) + dot(sk_n[k], parts[1]) + dot(sk_n[k], parts[2])
             put(dst, n, [g[:, c * BLK : (c + 1) * BLK] for c in range(3)], 3 * k)
 
-    spread(tire_pos, nscr, nb)
+    spread(s_tp, nscr, nb)
     tp = comps(nscr, nb)
     node_slots(tp, send1)
     send1[pl.ds(6, n, stride=8), :] = jnp.where(
@@ -294,8 +338,8 @@
 
     def send_edges(step):
         for u in range(2):
-            a = pscr[pl.ds(halo[2 * u] * 8, 8), :]
-            b = pscr[pl.ds(halo[2 * u + 1] * 8, 8), :]
+            a = pscr[pl.ds(s_halo[2 * u] * 8, 8), :]
+            b = pscr[pl.ds(s_halo[2 * u + 1] * 8, 8), :]
             edge[pl.ds((2 * step + u) * 8, 8), :] = jnp.concatenate(
                 [a[0:3], b[0:3], jnp.zeros((2, BLK), F32)], axis=0
             )
@@ -308,7 +352,8 @@
             device_id_type=MESH,
         ).start()
 
-    spread(part_pos, pscr, nt)
+    ready(3, 5)
+    spread(s_pp, pscr, nt)
     pp = comps(pscr, nt)
     tiles_split(pp)
     send_edges(0)
@@ -322,32 +367,38 @@
         out = [jnp.zeros((nt, BLK), F32) for _ in range(3)]
         for u in range(2):
             at = pl.ds((2 * step + u) * 8, 8)
-            force, unused = pair(edge[at, :], hrecv[at, :])
-            force = force * live
+            put_weights(ws, u, edge[at, :], hrecv[at, :])
+            push = push_of(ws, u, edge[at, :], hrecv[at, :]) * live
             for k in range(2):
-                here = sub_t == halo[2 * u + k]
+                here = sub_t == s_halo[2 * u + k]
                 for c in range(3):
                     r = 3 * k + c
-                    out[c] = out[c] + jnp.where(here, force[r : r + 1, :], 0.0)
+                    out[c] = out[c] + jnp.where(here, push[r : r + 1, :], 0.0)
         return out
 
+    for k in range(2):
+        sk_t[k] = jnp.transpose(sk_n[k].astype(F32)).astype(BF)
+    ready(5, 9)
     bcopy.wait()
 
     def split_block(q, c):
         for s in range(2):
-            b = bstage[2 * q + s]
+            b = jnp.transpose(bstage[2 * q + s])
             hi = b.astype(BF)
-            bsplit[q, s * BLK : (s + 1) * BLK, 0:BLK] = hi
-            bsplit[q, s * BLK : (s + 1) * BLK, BLK : 2 * BLK] = (
+            bsplit[q, 0:BLK, s * BLK : (s + 1) * BLK] = hi
+            bsplit[q, BLK : 2 * BLK, s * BLK : (s + 1) * BLK] = (
                 b - hi.astype(F32)
             ).astype(BF)
         return c
 
-    lax.fori_loop(0, nb // 2, split_block, 0)
-
-    cmat = jnp.zeros((nb, BLK), F32)
+    lax.fori_loop(0, nb // 2, split_block, 0, unroll=4)
+
+    cmat = jnp.zeros((BLK, nb), F32)
     for m in range(NNZB):
-        cmat = cmat + jnp.where(lane_b == pattern[:, m : m + 1], coup[:, m : m + 1], 0.0)
+        cmat = cmat + jnp.where(
+            sub_b == s_pattern[m : m + 1, :], s_coup[m : m + 1, :], 0.0
+        )
+    cmat = jnp.transpose(pad_lanes(cmat))[0:nb]
     c_hi = cmat.astype(BF)
     c_lo = (cmat - c_hi.astype(F32)).astype(BF)
     vs[...] = jnp.zeros_like(vs)
@@ -363,7 +414,7 @@
                 q = j * UNROLL + u
                 at = pl.ds(pl.multiple_of(q * 16, 16), 16)
                 t = vs[at, :].astype(BF)
-                o = dot_nt(jnp.concatenate([t, t], axis=1), bsplit[q])
+                o = dot(jnp.concatenate([t, t], axis=1), bsplit[q])
                 vo[at, :] = jnp.concatenate([o[0:8, :BLK], o[8:16, BLK:]], axis=0)
             return carry
 
@@ -403,6 +454,15 @@
 
     lane_g = lax.broadcasted_iota(jnp.int32, (GROUP, BLK), 1)
     lane_gm = (lane_g & (nt - 1)).astype(F32)
+
+    def pairs(g, near, far, push, react):
+        for u in range(GROUP):
+            at = tile_rows(g * GROUP + u)
+            put_weights(ws, u, near[at, :], far[at, :])
+        for u in range(GROUP):
+            at = tile_rows(g * GROUP + u)
+            react[at, :] = react_of(ws, u, near[at, :], far[at, :])
+            push[at, :] = push_of(ws, u, near[at, :], far[at, :])
 
     def owner_group(g, c):
         base = pl.multiple_of(g * GROUP * 8, GROUP * 8)
@@ -419,13 +479,12 @@
                     k * GROUP : (k + 1) * GROUP, cc * BLK : (cc + 1) * BLK
                 ]
 
-        def some(j, carry):
-            for u in range(UNROLL):
-                i = g * GROUP + j * UNROLL + u
-                at = tile_rows(i)
-                push1[at, :], react1[at, :] = pair(near1[at, :], far1[at, :])
-            for u in range(UNROLL):
-                i = g * GROUP + j * UNROLL + u
+        pairs(g, near1, far1, push1, react1)
+        for u in range(GROUP):
+            i = g * GROUP + u
+            if u > 0:
+                remote(push1, pret, i, 6, ssem.at[1], psem, behind(i))
+            else:
 
                 @pl.when(i > 0)
                 def _():
@@ -435,9 +494,6 @@
                 def _():
                     own(push1, pret, 6, psem)
 
-            return carry
-
-        lax.fori_loop(0, GROUP // UNROLL, some, 0)
         return c
 
     lax.fori_loop(0, n // GROUP, owner_group, 0)
@@ -450,7 +506,7 @@
 
     hf = halo_force(0)
     sf = soil_sum(react1)
-    spread(part_vel, pscr, nt)
+    spread(s_pv, pscr, nt)
     pv = comps(pscr, nt)
     pv = [pv[c] + time_step * (sf[c] + hf[c]) for c in range(3)]
     pp = [pp[c] + time_step * pv[c] for c in range(3)]
@@ -469,7 +525,7 @@
     lax.fori_loop(1, n, send_tiles, 0)
     send_edges(1)
 
-    spread(tire_vel, nscr, nb)
+    spread(s_tv, nscr, nb)
     tv = comps(nscr, nb)
     wait_rows(pret, psem, n, 6)
     nf = node_sum(pret)
@@ -480,13 +536,12 @@
     def node_group(g, c):
         wait_rows(tret, tsem.at[g], GROUP, 6)
 
-        def some(j, carry):
-            for u in range(UNROLL):
-                i = g * GROUP + j * UNROLL + u
-                at = tile_rows(i)
-                push2[at, :], react2[at, :] = pair(near2[at, :], tret[at, :])
-            for u in range(UNROLL):
-                i = g * GROUP + j * UNROLL + u
+        pairs(g, near2, tret, push2, react2)
+        for u in range(GROUP):
+            i = g * GROUP + u
+            if u > 0:
+                remote(react2, rret, i, 6, ssem.at[3], rrsem, ahead(i))
+            else:
 
                 @pl.when(i > 0)
                 def _():
@@ -496,9 +551,6 @@
                 def _():
                     own(react2, rret, 6, rrsem)
 
-            return carry
-
-        lax.fori_loop(0, GROUP // UNROLL, some, 0)
         return c
 
     lax.fori_loop(0, n // GROUP, node_group, 0)
@@ -527,6 +579,12 @@
     for step in range(2):
         view = edge.at[pl.ds(step * 16, 16), :]
         pltpu.make_async_copy(view, view, hssem.at[step]).wait()
+
+
+def hand_over(*refs):
+    count = len(refs) // 2
+    for k in range(count):
+        refs[count + k][...] = refs[k][...]
 
 
 def local(
@@ -546,20 +604,30 @@
     nb = tire_pos.shape[1] // BLK
     nt = part_pos.shape[1] // BLK
     vmem = pl.BlockSpec(memory_space=pltpu.VMEM)
-    smem = pl.BlockSpec(memory_space=pltpu.SMEM)
-    hbm = pl.BlockSpec(memory_space=pl.ANY)
+    hbm = pl.BlockSpec(memory_space=pltpu.HBM)
     message = pltpu.VMEM((n * 8, BLK), F32)
-    return pl.pallas_call(
+    outs = (
+        jax.ShapeDtypeStruct(tire_pos.shape, F32),
+        jax.ShapeDtypeStruct(tire_pos.shape, F32),
+        jax.ShapeDtypeStruct(part_pos.shape, F32),
+        jax.ShapeDtypeStruct(part_pos.shape, F32),
+    )
+    results = pl.pallas_call(
         functools.partial(kernel, n, n_dom, nb, nt),
-        out_shape=(
-            jax.ShapeDtypeStruct(tire_pos.shape, F32),
-            jax.ShapeDtypeStruct(tire_pos.shape, F32),
-            jax.ShapeDtypeStruct(part_pos.shape, F32),
-            jax.ShapeDtypeStruct(part_pos.shape, F32),
-        ),
-        in_specs=[vmem, vmem, vmem, vmem, vmem, vmem, smem, hbm, vmem, vmem],
+        out_shape=outs,
+        in_specs=[hbm] * 10,
         out_specs=[vmem] * 4,
         scratch_shapes=[
+            pltpu.VMEM(tire_pos.shape, F32),
+            pltpu.VMEM(tire_pos.shape, F32),
+            pltpu.VMEM(part_pos.shape, F32),
+            pltpu.VMEM(part_pos.shape, F32),
+            pltpu.VMEM((TOPC, nb), jnp.int32),
+            pltpu.VMEM((TOPC, nb), jnp.int32),
+            pltpu.SMEM((HB,), jnp.int32),
+            pltpu.VMEM((NNZB, nb), jnp.int32),
+            pltpu.VMEM((NNZB, nb), F32),
+            pltpu.VMEM((GROUP, 2 * BLK, 2 * BLK), BF),
             pltpu.VMEM((nb, BLK, BLK), F32),
             pltpu.VMEM((nb // 2, 2 * BLK, 2 * BLK), BF),
             pltpu.VMEM((nb * 8, BLK), F32),
@@ -577,6 +645,7 @@
             pltpu.VMEM((2, BLK, BLK), BF),
             pltpu.VMEM((2, BLK, BLK), BF),
             pltpu.VMEM((BLK, BLK), BF),
+            pltpu.SemaphoreType.DMA((9,)),
             pltpu.SemaphoreType.DMA,
             pltpu.SemaphoreType.DMA((4,)),
             pltpu.SemaphoreType.DMA((n // GROUP,)),
@@ -587,20 +656,27 @@
             pltpu.SemaphoreType.DMA((2,)),
         ],
         compiler_params=pltpu.CompilerParams(
-            collective_id=0, has_side_effects=True, vmem_limit_bytes=48 << 20
+            collective_id=0, has_side_effects=True, vmem_limit_bytes=62 << 20
         ),
     )(
         tire_pos,
         tire_vel,
         part_pos,
         part_vel,
-        contact_owner,
-        contact_tile,
+        contact_owner.T,
+        contact_tile.T,
         halo_tiles,
         block_inverse,
-        pattern,
-        coupling,
+        pattern.T,
+        coupling.T,
     )
+    return pl.pallas_call(
+        hand_over,
+        out_shape=outs,
+        in_specs=[vmem] * 4,
+        out_specs=[vmem] * 4,
+        compiler_params=pltpu.CompilerParams(vmem_limit_bytes=62 << 20),
+    )(*results)
 
 
 def solution(mesh):

time: 103 us -> 66.2 us (0.64)
  Pallas kernels: 92.1 us -> 65.4 us
  local copies, waits for them, and re-layouts: 10.1 us -> 0 us
    pallas_call x1 -> x2, Pallas kernels: 92.1 us -> 65.4 us  [the longest x1 63.4 us: local(): pl.pallas_call(functools.partial(kernel, n, n_dom, nb, nt), out_shape=out...]
    unnamed x18 -> x0, local copies, waits for them, and re-layouts: 10.1 us -> none
where the time goes in v2:
time: 66.2 us; the launch traced here: 66.1 us
  Pallas kernels  65.4 us (99%)
    pallas_call x1, Pallas kernels, local(): pl.pallas_call(functools.partial(kernel, n, n_dom, nb, nt), out_shape=out...  63.4 us
    pallas_call x1, Pallas kernels, local(): pl.pallas_call(hand_over, out_shape=outs, in_specs=[vmem] * 4, out_specs=...  2.05 us

profile of v2, /device:TPU:1, one launch (start us, length us, event | category | flops | bytes accessed | tf_op | source)
XLA Modules:
  0.0 66.1 jit_solution(76928546500211506)
XLA Ops:
  0.6 63.4 %shard_map.129 = (f32[3,12288]{1,0:T(4,128)}, f32[3,12288]{1,0:T(4,128)}, f32[3,8192]{1,0:T(4,128)}, f32[3,8192]{1,0:T(4,128)}) custom-call(f32[3,12288]{1,0:T(4,128)} %tire_pos.1, f32[3,12288]{1,0:T(4,128)} %tire_vel.1, f32[3,8192]{1,0:T(4,128)} %part_pos.1, f32[3,8192]{1,0:T(4,128)} %part_vel.1, s32[2,96]{1,0:T(2,128)} %bitcast.6, s32[2,96]{1,0:T(2,128)} %bitcast.7, ...), custom_call_target="tpu_custom_call" | custom-call | tf_op jit(solution)/shard_map/pallas_call | solution.py:615
  64.0 2.1 %shard_map.130 = (f32[3,12288]{1,0:T(4,128)}, f32[3,12288]{1,0:T(4,128)}, f32[3,8192]{1,0:T(4,128)}, f32[3,8192]{1,0:T(4,128)}) custom-call(f32[3,12288]{1,0:T(4,128)} %get-tuple-element.8.refs_0_, f32[3,12288]{1,0:T(4,128)} %get-tuple-element.9.refs_1_, f32[3,8192]{1,0:T(4,128)} %get-tuple-element.10.refs_2_, f32[3,8192]{1,0:T(4,128)} %get-tuple-element.11.refs_3_), custom_call_target="tpu_custom_call" | custom-call | tf_op jit(solution)/shard_map/pallas_call | solution.py:673

commit v3 on v2

--- a/solution.py
+++ b/solution.py
@@ -14,7 +14,6 @@
 SWEEPS = 3
 HB = 4
 GROUP = 16
-UNROLL = 16
 
 BF = jnp.bfloat16
 F32 = jnp.float32
@@ -409,16 +408,11 @@
             vs[pl.ds(c, nb, stride=8), :] = h
             vs[pl.ds(3 + c, nb, stride=8), :] = l
 
-        def some(j, carry):
-            for u in range(UNROLL):
-                q = j * UNROLL + u
-                at = pl.ds(pl.multiple_of(q * 16, 16), 16)
-                t = vs[at, :].astype(BF)
-                o = dot(jnp.concatenate([t, t], axis=1), bsplit[q])
-                vo[at, :] = jnp.concatenate([o[0:8, :BLK], o[8:16, BLK:]], axis=0)
-            return carry
-
-        lax.fori_loop(0, nb // 2 // UNROLL, some, 0)
+        for q in range(nb // 2):
+            at = pl.ds(q * 16, 16)
+            t = vs[at, :].astype(BF)
+            o = dot(jnp.concatenate([t, t], axis=1), bsplit[q])
+            vo[at, :] = jnp.concatenate([o[0:8, :BLK], o[8:16, BLK:]], axis=0)
         a, b = comps(vo, nb), comps(vo, nb, 3)
         return [a[c] + b[c] for c in range(3)]
 

time: 66.2 us -> 64 us (0.967)
  Pallas kernels: 65.4 us -> 63.2 us
    pallas_call x1, Pallas kernels: 63.4 us -> 61.1 us  [local(): pl.pallas_call(functools.partial(kernel, n, n_dom, nb, nt), out_shape=out...]
where the time goes in v3:
time: 64 us; the launch traced here: 63.8 us
  Pallas kernels  63.2 us (99%)
  between operations  0.64 us (1%)
    pallas_call x1, Pallas kernels, local(): pl.pallas_call(functools.partial(kernel, n, n_dom, nb, nt), out_shape=out...  61.1 us
    pallas_call x1, Pallas kernels, local(): pl.pallas_call(hand_over, out_shape=outs, in_specs=[vmem] * 4, out_specs=...  2.05 us

profile of v3, /device:TPU:1, one launch (start us, length us, event | category | flops | bytes accessed | tf_op | source)
XLA Modules:
  0.0 63.8 jit_solution(1285547611049725668)
XLA Ops:
  0.6 61.1 %shard_map.129 = (f32[3,12288]{1,0:T(4,128)}, f32[3,12288]{1,0:T(4,128)}, f32[3,8192]{1,0:T(4,128)}, f32[3,8192]{1,0:T(4,128)}) custom-call(f32[3,12288]{1,0:T(4,128)} %tire_pos.1, f32[3,12288]{1,0:T(4,128)} %tire_vel.1, f32[3,8192]{1,0:T(4,128)} %part_pos.1, f32[3,8192]{1,0:T(4,128)} %part_vel.1, s32[2,96]{1,0:T(2,128)} %bitcast.6, s32[2,96]{1,0:T(2,128)} %bitcast.7, ...), custom_call_target="tpu_custom_call" | custom-call | tf_op jit(solution)/shard_map/pallas_call | solution.py:609
  61.8 2.1 %shard_map.130 = (f32[3,12288]{1,0:T(4,128)}, f32[3,12288]{1,0:T(4,128)}, f32[3,8192]{1,0:T(4,128)}, f32[3,8192]{1,0:T(4,128)}) custom-call(f32[3,12288]{1,0:T(4,128)} %get-tuple-element.8.refs_0_, f32[3,12288]{1,0:T(4,128)} %get-tuple-element.9.refs_1_, f32[3,8192]{1,0:T(4,128)} %get-tuple-element.10.refs_2_, f32[3,8192]{1,0:T(4,128)} %get-tuple-element.11.refs_3_), custom_call_target="tpu_custom_call" | custom-call | tf_op jit(solution)/shard_map/pallas_call | solution.py:667

commit v4 on v3

--- a/solution.py
+++ b/solution.py
@@ -192,13 +192,13 @@
     me = lax.axis_index("role") * n_dom + lax.axis_index("dom")
 
     def dev(p):
-        return (p // n_dom, p % n_dom)
+        return (lax.div(p, n_dom), lax.rem(p, n_dom))
 
     def ahead(i):
-        return dev((me + i) % n)
+        return dev(lax.rem(me + i, n))
 
     def behind(i):
-        return dev((me + n - i) % n)
+        return dev(lax.rem(me + n - i, n))
 
     arrive = []
     for k, (src, dst) in enumerate(

time: 64 us -> 61.5 us (0.961)
  Pallas kernels: 63.2 us -> 60.8 us
    pallas_call x1, Pallas kernels: 61.1 us -> 58.7 us  [local(): pl.pallas_call(functools.partial(kernel, n, n_dom, nb, nt), out_shape=out...]
where the time goes in v4:
time: 61.5 us; the launch traced here: 61.4 us
  Pallas kernels  60.8 us (99%)
  between operations  0.64 us (1%)
    pallas_call x1, Pallas kernels, local(): pl.pallas_call(functools.partial(kernel, n, n_dom, nb, nt), out_shape=out...  58.7 us
    pallas_call x1, Pallas kernels, local(): pl.pallas_call(hand_over, out_shape=outs, in_specs=[vmem] * 4, out_specs=...  2.05 us

profile of v4, /device:TPU:1, one launch (start us, length us, event | category | flops | bytes accessed | tf_op | source)
XLA Modules:
  0.0 61.4 jit_solution(14209155939180388853)
XLA Ops:
  0.6 58.7 %shard_map.129 = (f32[3,12288]{1,0:T(4,128)}, f32[3,12288]{1,0:T(4,128)}, f32[3,8192]{1,0:T(4,128)}, f32[3,8192]{1,0:T(4,128)}) custom-call(f32[3,12288]{1,0:T(4,128)} %tire_pos.1, f32[3,12288]{1,0:T(4,128)} %tire_vel.1, f32[3,8192]{1,0:T(4,128)} %part_pos.1, f32[3,8192]{1,0:T(4,128)} %part_vel.1, s32[2,96]{1,0:T(2,128)} %bitcast.6, s32[2,96]{1,0:T(2,128)} %bitcast.7, ...), custom_call_target="tpu_custom_call" | custom-call | tf_op jit(solution)/shard_map/pallas_call | solution.py:609
  59.4 2.1 %shard_map.130 = (f32[3,12288]{1,0:T(4,128)}, f32[3,12288]{1,0:T(4,128)}, f32[3,8192]{1,0:T(4,128)}, f32[3,8192]{1,0:T(4,128)}) custom-call(f32[3,12288]{1,0:T(4,128)} %get-tuple-element.8.refs_0_, f32[3,12288]{1,0:T(4,128)} %get-tuple-element.9.refs_1_, f32[3,8192]{1,0:T(4,128)} %get-tuple-element.10.refs_2_, f32[3,8192]{1,0:T(4,128)} %get-tuple-element.11.refs_3_), custom_call_target="tpu_custom_call" | custom-call | tf_op jit(solution)/shard_map/pallas_call | solution.py:667
